TPU v7x, 512 devices: a whole 4x4x16 slice. The times are simulated.
512 devices in a mesh: ctx: 16 (over z), rep: 32 (over x, y, core).
Axes of the slice: x: 4, y: 4, z: 16, core: 2. Of those that a mesh axis runs over, the one named last changes fastest.
Arguments:
- cache_keys: bfloat16 [32, 65536, 128], P('rep', 'ctx'), may hold values from -8 to 8
- cache_values: bfloat16 [32, 65536, 128], P('rep', 'ctx'), may hold values from -6 to 6
- query_pool: bfloat16 [32, 4096, 128], P('rep', 'ctx'), may hold values from -8 to 8
- kept_index: int32 [32, 4096], P('rep', 'ctx'), may hold values from 0 to 65535, as said below
- ref_index: int32 [32, 512], P('rep'), may hold values from 0 to 4095, as said below
Outputs:
- fitted_values: float32 [32, 4096, 128], P('rep', 'ctx')
Inputs may be any that keep to these rules, and one draw needn't show every extreme that they name: `kept_index`: for each pair, the 256 kept slots of block c name distinct positions of cache block c, c * 4096 to (c + 1) * 4096 - 1. `ref_index`: distinct within each pair.
All inputs are finite; a program needn't handle non-finite values.
Results may differ from a plain program's by a relative error of at most 0.0003.
Values may be sent and summed in bfloat16 or wider, within the bound.
A program may use at most 64 MiB of HBM per device.

v0:
```python
import math

import jax
import jax.numpy as jnp
from jax import lax
from jax.sharding import PartitionSpec as P

ITERS = 3


def merged_2(array, axis, combine):
    everything = jax.tree.map(lambda part: lax.all_gather(part, axis), array)
    first = jax.tree.map(lambda part: part[0], everything)

    def hop(k, so_far):
        return combine(so_far, jax.tree.map(lambda part: part[k], everything))

    return lax.fori_loop(1, lax.axis_size(axis), hop, first)


def softmax_combine(first, second):
    top = jnp.maximum(first[0], second[0])
    left = jnp.exp(first[0] - top)
    right = jnp.exp(second[0] - top)
    return (
        top,
        first[1] * left + second[1] * right,
        first[2] * left[:, None] + second[2] * right[:, None],
    )


def local(cache_keys, cache_values, query_pool, kept_index, ref_index):
    highest = lax.Precision.HIGHEST
    shards = lax.axis_size("ctx")
    here = lax.axis_index("ctx")
    ctx_rows = cache_keys.shape[1]
    head_size = cache_keys.shape[2]
    scale = 1.0 / head_size**0.5
    kept_count = kept_index.shape[1] * shards
    query_count = ref_index.shape[1]
    ridge = 0.3 * query_count / (kept_count * kept_count)
    pool = lax.all_gather(query_pool, "ctx", axis=1, tiled=True)[0]
    queries = jnp.take(pool, ref_index[0], axis=0)
    key_rows = cache_keys[0]
    value_rows = cache_values[0]
    block = math.gcd(ctx_rows, 1024)
    key_blocks = key_rows.reshape(ctx_rows // block, block, head_size)
    value_blocks = value_rows.reshape(ctx_rows // block, block, head_size)

    def find_top(carry, piece):
        scores = jnp.dot(queries, piece.T, preferred_element_type=jnp.float32)
        return (jnp.maximum(carry, jnp.max(scores, axis=1) * scale), None)

    start_top = jnp.full((query_count,), -jnp.inf, jnp.float32)
    maxima, unused = lax.scan(find_top, start_top, key_blocks)

    def accumulate(carry, pieces):
        scores = jnp.dot(queries, pieces[0].T, preferred_element_type=jnp.float32) * scale
        expo = jnp.exp(scores - maxima[:, None])
        weighted = jnp.dot(expo.astype(jnp.bfloat16), pieces[1], preferred_element_type=jnp.float32)
        return ((carry[0] + jnp.sum(expo, axis=1), carry[1] + weighted), None)

    start_sums = (
        jnp.zeros((query_count,), jnp.float32),
        jnp.zeros((query_count, head_size), jnp.float32),
    )
    sums, unused = lax.scan(accumulate, start_sums, (key_blocks, value_blocks))
    totals, weighted = sums
    local_kept = kept_index[0] - here * ctx_rows
    kept_keys = jnp.take(key_rows, local_kept, axis=0)
    kept_vals = jnp.take(value_rows, local_kept, axis=0).astype(jnp.float32)
    kept_scores = jnp.dot(queries, kept_keys.T, preferred_element_type=jnp.float32) * scale
    local_top = jnp.max(kept_scores, axis=1)
    merged = merged_2((maxima, totals, weighted), "ctx", softmax_combine)
    kept_top = lax.pmax(local_top, "ctx")
    expo = jnp.exp(kept_scores - kept_top[:, None])
    kept_total = lax.psum(jnp.sum(expo, axis=1), "ctx")
    target = merged[2] / merged[1][:, None]
    attend = expo / kept_total[:, None]
    start_image = lax.psum(jnp.dot(attend, kept_vals, precision=highest), "ctx")
    fitted = kept_vals
    residual = jnp.dot(attend.T, target - start_image, precision=highest)

    def column_norms(matrix):
        return lax.psum(jnp.sum(matrix * matrix, axis=0), "ctx")

    direction = residual
    norm_now = column_norms(residual)
    for step in range(ITERS):
        image, dir_norm = lax.psum(
            (jnp.dot(attend, direction, precision=highest), jnp.sum(direction * direction, axis=0)),
            "ctx",
        )
        curve = jnp.sum(image * image, axis=0) + ridge * dir_norm
        alpha = norm_now / curve
        fitted = fitted + alpha * direction
        residual = residual - alpha * (
            jnp.dot(attend.T, image, precision=highest) + ridge * direction
        )
        norm_next = column_norms(residual)
        direction = residual + norm_next / norm_now * direction
        norm_now = norm_next
    return fitted[None]


def solution(mesh):
    placed = (
        P("rep", "ctx", None),
        P("rep", "ctx", None),
        P("rep", "ctx", None),
        P("rep", "ctx"),
        P("rep", None),
    )
    return jax.shard_map(
        local, mesh=mesh, in_specs=placed, out_specs=P("rep", "ctx", None), check_vma=False
    )
```

profile of v0, /device:TPU:2, one launch (start us, length us, event | category | flops | bytes accessed | tf_op | source)
XLA Modules:
  0.0 825.0 jit_solution(6367981897641551951)
XLA Ops:
  8.7 76.2 %all-gather.8.cloned.1.call-done = bf16[1,4096,128]{2,1,0:T(8,128)(2,1)} async-done(((bf16[1,256,128]{2,1,0:T(8,128)(2,1)}), bf16[1,4096,128]{2,1,0:T(8,128)(2,1)}) %all-gather.8.cloned.1.call-update) | async-done | bytes 1048592 | tf_op jit(solution)/shard_map/all_gather | solution.py:42
  84.9 2.4 gather_fusion
  87.5 5.8 while.44
  87.5 1.5 convolution_reduce_fusion.2
  89.1 1.4 convolution_reduce_fusion.2
  90.5 1.4 convolution_reduce_fusion.2
  93.4 8.3 %while.45 = (s32[]{:T(128)}, f32[512]{0:T(512)S(1)}, f32[512,128]{1,0:T(8,128)S(1)}, bf16[4,1024,128]{2,1,0:T(8,128)(2,1)}, bf16[512,128]{1,0:T(8,128)(2,1)S(1)}...) while((s32[]{:T(128)}, f32[512]{0:T(512)S(1)}, ...), condition=%wide.region_9.11_spmd.clone, body=%wide.region_7.10_spmd.clone.sunk | while | flops 271712768 | bytes 5386360 | solution.py:67
  93.4 1.5 fusion.64
  95.5 1.5 fusion.64
  97.5 1.5 fusion.64
  99.6 1.5 fusion.64
  103.4 2.1 gather_fusion.2
  105.5 28.8 %all-gather.3 = f32[16,1,512]{2,1,0:T(1,128)S(1)} all-gather(f32[1,1,512]{2,1,0:T(1,128)S(1)} %bitcast.69), channel_id=2, replica_groups=mesh['ctx'=16,'rep'=32] {'ctx'}, dimensions={0}, use_global_device_ids=true | all-gather | bytes 34816 | tf_op jit(solution)/shard_map/all_gather | solution.py:12
  134.2 26.1 %all-gather.4 = f32[16,1,512]{2,1,0:T(1,128)S(1)} all-gather(f32[1,1,512]{2,1,0:T(1,128)S(1)} %bitcast.72), channel_id=3, replica_groups=mesh['ctx'=16,'rep'=32] {'ctx'}, dimensions={0}, use_global_device_ids=true | all-gather | bytes 34816 | tf_op jit(solution)/shard_map/all_gather | solution.py:12
  160.6 29.0 %pmax.7 = f32[512]{0:T(512)S(1)} all-reduce(f32[512]{0:T(512)S(1)} %get-tuple-element.333), channel_id=1, replica_groups=mesh['ctx'=16,'rep'=32] {'ctx'}, use_global_device_ids=true, to_apply=%region_1.3 | all-reduce | flops 512 | bytes 4096 | tf_op jit(solution)/shard_map/pmax | solution.py:75
  189.8 27.0 %psum.73 = f32[512]{0:T(512)S(1)} all-reduce(f32[512]{0:T(512)S(1)} %fusion.22), channel_id=1, replica_groups=mesh['ctx'=16,'rep'=32] {'ctx'}, use_global_device_ids=true, to_apply=%region_3.5 | all-reduce | flops 512 | bytes 4096 | tf_op jit(solution)/shard_map/psum | solution.py:77
  219.2 19.1 %while.43 = (s32[]{:T(128)}, f32[512]{0:T(512)S(1)}, f32[512]{0:T(512)S(1)}, f32[512,128]{1,0:T(8,128)S(1)}, f32[16,512]{1,0:T(8,128)S(1)}, /*index=5*/f32[16,51...) while((s32[]{:T(128)}, f32[512]{0:T(512)S(1)}, f32[512]{0:T(512)S(1)}, ...), condition=%wide.region_11.13_spmd, body=%wide.region_10.12_spmd.sunk | while | flops 199685 | bytes 815247 | solution.py:18
  238.3 111.9 %all-reduce.5.cloned.1.call-done = f32[512,128]{1,0:T(8,128)} async-done(((f32[512,128]{1,0:T(8,128)}), f32[512,128]{1,0:T(8,128)}) %all-reduce.5.cloned.1.call-update) | async-done | bytes 262160 | tf_op jit(solution)/shard_map/psum | solution.py:80
  350.2 1.6 multiply_reduce_fusion.7
  351.8 1.7 fusion.39
  353.6 29.4 %psum.75 = f32[128]{0:T(128)S(1)} all-reduce(f32[128]{0:T(128)S(1)} %get-tuple-element.335), channel_id=1, replica_groups=mesh['ctx'=16,'rep'=32] {'ctx'}, use_global_device_ids=true, to_apply=%region_14.16 | all-reduce | flops 128 | bytes 1024 | tf_op jit(solution)/shard_map/psum | solution.py:85
  383.0 102.9 %all-reduce.7.cloned.1.call-done = f32[512,128]{1,0:T(8,128)} async-done(((f32[512,128]{1,0:T(8,128)}), f32[512,128]{1,0:T(8,128)}) %all-reduce.7.cloned.1.call-update) | async-done | bytes 262160 | tf_op jit(solution)/shard_map/psum | solution.py:90
  487.0 1.6 multiply_reduce_fusion.6
  488.6 29.4 %psum.77 = f32[128]{0:T(128)S(1)} all-reduce(f32[128]{0:T(128)S(1)} %get-tuple-element.337), channel_id=1, replica_groups=mesh['ctx'=16,'rep'=32] {'ctx'}, use_global_device_ids=true, to_apply=%region_18.20 | all-reduce | flops 128 | bytes 1024 | tf_op jit(solution)/shard_map/psum | solution.py:85
  518.1 1.7 fusion.36
  519.8 27.0 %psum.79 = f32[128]{0:T(128)S(1)} all-reduce(f32[128]{0:T(128)S(1)} %get-tuple-element.327), channel_id=1, replica_groups=mesh['ctx'=16,'rep'=32] {'ctx'}, use_global_device_ids=true, to_apply=%region_22.24 | all-reduce | flops 128 | bytes 1024 | tf_op jit(solution)/shard_map/psum | solution.py:90
  546.9 104.3 %all-reduce.9.cloned.1.call-done = f32[512,128]{1,0:T(8,128)} async-done(((f32[512,128]{1,0:T(8,128)}), f32[512,128]{1,0:T(8,128)}) %all-reduce.9.cloned.1.call-update) | async-done | bytes 262160 | tf_op jit(solution)/shard_map/psum | solution.py:90
  652.2 1.6 multiply_reduce_fusion.4
  653.8 29.4 %psum.80 = f32[128]{0:T(128)S(1)} all-reduce(f32[128]{0:T(128)S(1)} %get-tuple-element.339), channel_id=1, replica_groups=mesh['ctx'=16,'rep'=32] {'ctx'}, use_global_device_ids=true, to_apply=%region_24.26 | all-reduce | flops 128 | bytes 1024 | tf_op jit(solution)/shard_map/psum | solution.py:85
  683.2 1.7 fusion.29
  685.0 27.0 %psum.82 = f32[128]{0:T(128)S(1)} all-reduce(f32[128]{0:T(128)S(1)} %multiply_reduce_fusion.3), channel_id=1, replica_groups=mesh['ctx'=16,'rep'=32] {'ctx'}, use_global_device_ids=true, to_apply=%region_28.30 | all-reduce | flops 128 | bytes 1024 | tf_op jit(solution)/shard_map/psum | solution.py:90
  712.1 104.3 %all-reduce.11.cloned.1.call-done = f32[512,128]{1,0:T(8,128)} async-done(((f32[512,128]{1,0:T(8,128)}), f32[512,128]{1,0:T(8,128)}) %all-reduce.11.cloned.1.call-update) | async-done | bytes 262160 | tf_op jit(solution)/shard_map/psum | solution.py:90
  (108 shorter events, 33.1 us)
Async XLA Ops:
  6.5 78.4 %all-gather.8.cloned.1.call-start = ((), (), s32[]{:S(2)}) async-start(), calls=%async_computation | async-start | bytes 1114112 | tf_op jit(solution)/shard_map/all_gather | solution.py:42
  7.3 211.0 %all-gather.10.cloned.1.call-start = ((), (), s32[]{:S(2)}) async-start(), calls=%async_computation.5 | async-start | bytes 4456448 | tf_op jit(solution)/shard_map/all_gather | solution.py:12
  87.4 6.0 copy-start.1
  93.4 9.1 %copy-start.2 = (s32[1,256]{1,0:T(1,128)S(1)}, s32[1,256]{1,0:T(1,128)}, u32[]{:S(2)}) copy-start(s32[1,256]{1,0:T(1,128)} %param.16) | copy-start | bytes 3076
  101.7 0.7 copy-start
  102.4 247.8 %all-reduce.5.cloned.1.call-start = ((), (), s32[]{:S(2)}) async-start(), calls=%async_computation.1 | async-start | bytes 524288 | tf_op jit(solution)/shard_map/psum | solution.py:80
  218.2 267.8 %all-reduce.7.cloned.1.call-start = ((), (), s32[]{:S(2)}) async-start(), calls=%async_computation.2 | async-start | bytes 524288 | tf_op jit(solution)/shard_map/psum | solution.py:90
  353.5 297.6 %all-reduce.9.cloned.1.call-start = ((), (), s32[]{:S(2)}) async-start(), calls=%async_computation.3 | async-start | bytes 524288 | tf_op jit(solution)/shard_map/psum | solution.py:90
  519.8 296.6 %all-reduce.11.cloned.1.call-start = ((), (), s32[]{:S(2)}) async-start(), calls=%async_computation.4 | async-start | bytes 524288 | tf_op jit(solution)/shard_map/psum | solution.py:90
Sparse Core Ops, SparseCore 0:
  9.4 75.4 all-gather.7
  102.5 75.7 all-gather.9
  218.3 131.8 all-reduce.4
  353.7 132.2 all-reduce.6
  519.9 131.2 all-reduce.8
  685.1 131.2 all-reduce.10
where the time goes:
time: 826 us; the launch traced here: 825 us
  waiting for transfers between devices  500 us (61%)
  blocking collectives  253 us (31%)
  matrix products  25.4 us (3%)
  other arithmetic  24.2 us (3%)
  between operations  13.6 us (2%)
    psum x3, waiting for transfers between devices, local(): lax.psum((jnp.dot(attend, direction, precision=highest), jnp.sum(directio...  312 us
    psum x1, waiting for transfers between devices, local(): start_image = lax.psum(jnp.dot(attend, kept_vals, precision=highest), 'ctx')  112 us
    psum x3, blocking collectives, column_norms(): return lax.psum(jnp.sum(matrix * matrix, axis=0), 'ctx')  88.3 us
    all_gather x1, waiting for transfers between devices, local(): pool = lax.all_gather(query_pool, 'ctx', axis=1, tiled=True)[0]  76.2 us
    all_gather x2, blocking collectives, merged_2(): everything = jax.tree.map(lambda part: lax.all_gather(part, axis), array)  54.9 us
    psum x2, blocking collectives, local(): lax.psum((jnp.dot(attend, direction, precision=highest), jnp.sum(directio...  54.1 us
    pmax x1, blocking collectives, local(): kept_top = lax.pmax(local_top, 'ctx')  29 us
    psum x1, blocking collectives, local(): kept_total = lax.psum(jnp.sum(expo, axis=1), 'ctx')  27 us
  transfers between devices with their start and end apart: 6, of which 5 were waited for; matrix products, arithmetic and copies ran while one was open for 3% of the time, Pallas kernels for 0%

commit v1 on v0

v1 whole, which is shorter than its diff:
```python
import functools

import jax
import jax.numpy as jnp
from jax import lax
from jax.experimental import pallas as pl
from jax.experimental.pallas import tpu as pltpu
from jax.sharding import PartitionSpec as P

ITERS = 3
HALVES = 2
F32 = jnp.float32
BF16 = jnp.bfloat16
MESH = pl.DeviceIdType.MESH


def nt(a, b):
    return lax.dot_general(a, b, (((1,), (1,)), ((), ())), preferred_element_type=F32)


def nn(a, b):
    return lax.dot_general(a, b, (((1,), (0,)), ((), ())), preferred_element_type=F32)


def split(x):
    high = x.astype(BF16)
    return high, (x - high.astype(F32)).astype(BF16)


def kernel(
    n, keys_hbm, vals_hbm, pool_ref, kept_ref, ref_ref, out_ref,
    keys, vals, vals_t, q_part, q_recv, q_blk, q_all, kk, v_t, v_recv,
    s_buf, p_t, stats, p_recv, stats_recv, a_buf, top_buf, a_high, a_low, gram, res, fin,
    load_sem, q_send, q_got, g_send, g_got, ring_send, ring_got, v_send, v_got,
    p_send, p_got, st_send, st_got, f_send, f_got,
):
    me = lax.axis_index("ctx")
    rows, head = keys.shape
    kept = kk.shape[1]
    queries = q_all.shape[0]
    half = queries // HALVES
    blk = half // n
    cols = head // n
    scale = 1.0 / head**0.5
    ridge = 0.3 * queries / ((kept * n) * (kept * n))

    def peer(d):
        return {"ctx": lax.rem(me + d, n)}

    def far_first(i):
        return n // 2 + (1 - 2 * (i % 2)) * ((i + 1) // 2)

    def sends(make):
        def body(i, carry):
            make(far_first(i)).start()
            return carry

        lax.fori_loop(0, n - 1, body, 0)

    def remote(src, dst, send, got, d):
        return pltpu.make_async_remote_copy(
            src_ref=src, dst_ref=dst, send_sem=send, recv_sem=got, device_id=peer(d), device_id_type=MESH
        )

    barrier = pltpu.get_barrier_semaphore()

    def greet(d, carry):
        pl.semaphore_signal(barrier, inc=1, device_id=peer(d), device_id_type=MESH)
        return carry

    lax.fori_loop(1, n, greet, 0)

    load_keys = pltpu.make_async_copy(keys_hbm.at[0], keys, load_sem.at[0])
    load_vals = pltpu.make_async_copy(vals_hbm.at[0], vals, load_sem.at[1])
    load_keys.start()
    load_vals.start()

    wanted = ref_ref[...] - me * pool_ref.shape[1]
    hit = lax.broadcasted_iota(jnp.int32, (pool_ref.shape[1], queries), 0) == wanted
    hit_t = jnp.where(hit, 1.0, 0.0).astype(F32).T.astype(BF16)
    q_part[...] = nn(hit_t, pool_ref[0]).astype(BF16)

    local = kept_ref[...] - me * rows
    local_col = jnp.broadcast_to(local, (128, kept)).T
    load_keys.wait()
    load_vals.wait()
    step = 512

    def pick(i, carry):
        at = pl.ds(pl.multiple_of(i * step, step), step)
        base = lax.broadcasted_iota(jnp.int32, (kept, 128), 1) + i * step
        hot = jnp.concatenate(
            [jnp.where(local_col == base + 128 * j, 1.0, 0.0).astype(BF16) for j in range(step // 128)], axis=1
        )
        vals_t[:, at] = vals[at, :].astype(F32).T.astype(BF16)
        return carry[0] + nn(hot, keys[at, :]), carry[1] + nn(hot, vals[at, :])

    zero = jnp.zeros((kept, head), F32)
    kept_keys, kept_vals = lax.fori_loop(0, rows // step, pick, (zero, zero))
    kk[0] = kept_keys.astype(BF16)
    v_t[...] = kept_vals.T

    pl.semaphore_wait(barrier, n - 1)

    for h in range(HALVES):

        def send_share(d, h=h):
            own = pl.ds(pl.multiple_of(h * half + lax.rem(me + d, n) * blk, blk), blk)
            return remote(q_part.at[own], q_recv.at[h, d], q_send.at[h], q_got.at[h], d)

        sends(send_share)
        mine = pl.ds(pl.multiple_of(h * half + me * blk, blk), blk)
        q_recv[h, 0] = q_part[mine, :]

    def ring(way, s):
        slot = s if way == 0 else lax.rem(n - s, n)
        there = s + 1 if way == 0 else n - s - 1
        return remote(
            kk.at[slot], kk.at[there], ring_send.at[way, s], ring_got.at[way, s], 1 if way == 0 else n - 1
        )

    right_steps, left_steps = n // 2, n - 1 - n // 2

    def ring_next(s):
        if s > 0:
            if s <= right_steps:
                ring(0, s - 1).wait_recv()
            if s <= left_steps:
                ring(1, s - 1).wait_recv()
        if s < right_steps:
            ring(0, s).start()
        if s < left_steps:
            ring(1, s).start()

    ring_next(0)

    for h in range(HALVES):
        if h == 1:
            ring_next(1)
        got = q_recv.at[h, pl.ds(1, n - 1)]
        pltpu.make_async_copy(got, got, q_got.at[h]).wait()
        total = q_recv[h, 0].astype(F32)
        for d in range(1, n):
            total = total + q_recv[h, d].astype(F32)
        q_blk[h] = total.astype(BF16)
        mine = pl.ds(pl.multiple_of(h * half + me * blk, blk), blk)

        def send_block(d, h=h, mine=mine):
            return remote(q_blk.at[h], q_all.at[mine], g_send.at[h], g_got.at[h], d)

        sends(send_block)
        q_all[mine, :] = q_blk[h]

    def send_vals(d):
        own = pl.ds(pl.multiple_of(lax.rem(me + d, n) * cols, cols), cols)
        return remote(v_t.at[own], v_recv.at[d], v_send, v_got, d)

    sends(send_vals)
    v_recv[0] = v_t[pl.ds(pl.multiple_of(me * cols, cols), cols), :]
    ring_next(2)
    ring_next(3)

    for h in range(HALVES):
        got = q_all.at[pl.ds(0, (n - 1) * blk)]
        pltpu.make_async_copy(got, got, g_got.at[h]).wait()
        q_half = q_all[h * half : (h + 1) * half, :]

        def score(i, top):
            at = pl.ds(pl.multiple_of(i * step, step), step)
            s = nt(keys[at, :], q_half) * scale
            s_buf[at, :] = s
            return jnp.maximum(top, jnp.max(s.reshape(step // 8, 8, half), axis=0))

        top = lax.fori_loop(0, rows // step, score, jnp.full((8, half), -jnp.inf, F32))
        top = jnp.max(top, axis=0, keepdims=True)

        def weigh(i, carry):
            at = pl.ds(pl.multiple_of(i * step, step), step)
            e = jnp.exp(s_buf[at, :] - top)
            total = carry[0] + jnp.sum(e.reshape(step // 8, 8, half), axis=0)
            return total, carry[1] + nn(vals_t[:, at], e.astype(BF16))

        total, weighted = lax.fori_loop(
            0, rows // step, weigh, (jnp.zeros((8, half), F32), jnp.zeros((head, half), F32))
        )
        total = jnp.sum(total, axis=0, keepdims=True)
        p_t[h] = weighted
        for j in range(half // 128):
            stats[h, j : j + 1, :] = top[:, j * 128 : (j + 1) * 128]
            stats[h, 2 + j : 3 + j, :] = total[:, j * 128 : (j + 1) * 128]

        def send_weighted(d, h=h):
            own = pl.ds(pl.multiple_of(lax.rem(me + d, n) * cols, cols), cols)
            return remote(p_t.at[h, own], p_recv.at[h, d], p_send.at[h], p_got.at[h], d)

        def send_stats(d, h=h):
            return remote(stats.at[h], stats_recv.at[h, d], st_send.at[h], st_got.at[h], d)

        sends(send_stats)
        sends(send_weighted)
        p_recv[h, 0] = p_t[h, pl.ds(pl.multiple_of(me * cols, cols), cols), :]
        stats_recv[h, 0] = stats[h]
        ring_next(4 + h)

    q_now = q_all[...]
    top_buf[...] = jnp.full(top_buf.shape, -jnp.inf, F32)

    def kept_scores(slot):
        s = nt(q_now, kk[slot]) * scale
        a_buf[:, pl.ds(pl.multiple_of(slot * kept, kept), kept)] = s
        best = top_buf[...]
        for j in range(kept // 128):
            best = jnp.maximum(best, s[:, j * 128 : (j + 1) * 128])
        top_buf[...] = best

    def kept_scores_body(slot, carry):
        kept_scores(slot)
        return carry

    done_right, done_left = 5, 5
    lax.fori_loop(0, done_right + 1, kept_scores_body, 0)
    lax.fori_loop(n - done_left, n, kept_scores_body, 0)
    for s in range(6, right_steps + 1):
        ring_next(s)
        kept_scores(s)
        if s <= left_steps:
            kept_scores(n - s)
    best = jnp.max(top_buf[...], axis=1, keepdims=True)
    top_buf[...] = jnp.broadcast_to(best, top_buf.shape)

    def kept_weights(i, carry):
        at = pl.ds(pl.multiple_of(i * 128, 128), 128)
        high, low = split(jnp.exp(a_buf[:, at] - top_buf[...]))
        a_high[:, at] = high
        a_low[:, at] = low
        return carry

    lax.fori_loop(0, n * kept // 128, kept_weights, 0)

    got = v_recv.at[pl.ds(1, n - 1)]
    pltpu.make_async_copy(got, got, v_got).wait()
    vals_here = jnp.concatenate([v_recv[d] for d in range(n)], axis=1)
    rows_aug = jnp.concatenate([vals_here, jnp.ones_like(vals_here)], axis=0).astype(BF16)
    fitted_now = nt(rows_aug, a_high[...]) + nt(rows_aug, a_low[...])
    inverse = 1.0 / fitted_now[cols : cols + 1, :]
    fitted_now = fitted_now[:cols, :] * inverse

    def products(i, carry):
        at = pl.ds(pl.multiple_of(i * 256, 256), 256)
        gram[:, at] = nt(a_high[...], a_low[at, :])
        return carry

    lax.fori_loop(0, queries // 256, products, 0)
    gram[...] = gram[...] + gram[...].T

    def squares(i, carry):
        at = pl.ds(pl.multiple_of(i * 256, 256), 256)
        gram[:, at] = gram[:, at] + nt(a_high[...], a_high[at, :])
        return carry

    lax.fori_loop(0, queries // 256, squares, 0)
    gram_high, gram_low = split(gram[...])

    pieces = []
    for h in range(HALVES):
        got = stats_recv.at[h, pl.ds(1, n - 1)]
        pltpu.make_async_copy(got, got, st_got.at[h]).wait()
        got = p_recv.at[h, pl.ds(1, n - 1)]
        pltpu.make_async_copy(got, got, p_got.at[h]).wait()
        for j in range(half // 128):
            tops = stats_recv[h, :, j : j + 1, :]
            totals = stats_recv[h, :, 2 + j : 3 + j, :]
            factor = jnp.exp(tops - jnp.max(tops, axis=0, keepdims=True))
            weighted = jnp.sum(factor * p_recv[h, :, :, j * 128 : (j + 1) * 128], axis=0)
            pieces.append(weighted / jnp.sum(factor * totals, axis=0))
    target = jnp.concatenate(pieces, axis=1)

    def apply(x):
        high, low = split(x * inverse)
        both = nn(jnp.concatenate([high, low], axis=0), gram_high)
        return (both[:cols] + both[cols:] + nn(high, gram_low)) * inverse

    def dots(a, b):
        return jnp.sum(a * b, axis=1, keepdims=True)

    y = target - fitted_now
    image_y = apply(y)
    norm_now = dots(y, image_y)
    u, image = y, image_y
    answer = jnp.zeros_like(y)
    for it in range(ITERS):
        curve = dots(image, image) + ridge * dots(u, image)
        alpha = norm_now / curve
        answer = answer + alpha * u
        if it == ITERS - 1:
            break
        y = y - alpha * (image + ridge * u)
        image_y = apply(y)
        norm_next = dots(y, image_y)
        beta = norm_next / norm_now
        u = y + beta * u
        image = image_y + beta * image
        norm_now = norm_next

    high, low = split(answer * inverse)
    both_ways = jnp.concatenate([high, low], axis=0)
    own_cols = pl.ds(pl.multiple_of(me * cols, cols), cols)

    def result(slot):
        at = pl.ds(pl.multiple_of(slot * kept, kept), kept)
        both = nn(both_ways, a_high[:, at])
        return v_recv[slot] + both[:cols] + both[cols:] + nn(high, a_low[:, at])

    def give(i, carry):
        d = far_first(i)
        res[d] = result(n - d)
        remote(res.at[d], fin.at[own_cols], f_send, f_got, d).start()
        return carry

    lax.fori_loop(0, n - 1, give, 0)
    fin[own_cols, :] = result(0)

    def drain(ref, sem):
        pltpu.make_async_copy(ref, ref, sem).wait()

    for h in range(HALVES):
        drain(q_recv.at[h, pl.ds(1, n - 1)], q_send.at[h])
        drain(q_all.at[pl.ds(0, (n - 1) * blk)], g_send.at[h])
        drain(p_recv.at[h, pl.ds(1, n - 1)], p_send.at[h])
        drain(stats_recv.at[h, pl.ds(1, n - 1)], st_send.at[h])
    drain(v_recv.at[pl.ds(1, n - 1)], v_send)
    for s in range(right_steps):
        ring(0, s).wait_send()
        if s < left_steps:
            ring(1, s).wait_send()
    drain(res.at[pl.ds(1, n - 1)], f_send)
    drain(res.at[pl.ds(1, n - 1)], f_got)
    out_ref[0] = fin[...].T


def local(cache_keys, cache_values, query_pool, kept_index, ref_index):
    n = lax.axis_size("ctx")
    rows, head = cache_keys.shape[1:]
    kept = kept_index.shape[1]
    queries = ref_index.shape[1]
    half = queries // HALVES
    blk = half // n
    cols = head // n
    vmem = pl.BlockSpec(memory_space=pltpu.VMEM)
    hbm = pl.BlockSpec(memory_space=pl.ANY)
    dma = pltpu.SemaphoreType.DMA
    return pl.pallas_call(
        functools.partial(kernel, n),
        out_shape=jax.ShapeDtypeStruct((1, kept, head), F32),
        in_specs=[hbm, hbm, vmem, vmem, vmem],
        out_specs=vmem,
        scratch_shapes=[
            pltpu.VMEM((rows, head), BF16),
            pltpu.VMEM((rows, head), BF16),
            pltpu.VMEM((head, rows), BF16),
            pltpu.VMEM((queries, head), BF16),
            pltpu.VMEM((HALVES, n, blk, head), BF16),
            pltpu.VMEM((HALVES, blk, head), BF16),
            pltpu.VMEM((queries, head), BF16),
            pltpu.VMEM((n, kept, head), BF16),
            pltpu.VMEM((head, kept), F32),
            pltpu.VMEM((n, cols, kept), F32),
            pltpu.VMEM((rows, half), F32),
            pltpu.VMEM((HALVES, head, half), F32),
            pltpu.VMEM((HALVES, 4, 128), F32),
            pltpu.VMEM((HALVES, n, cols, half), F32),
            pltpu.VMEM((HALVES, n, 4, 128), F32),
            pltpu.VMEM((queries, n * kept), F32),
            pltpu.VMEM((queries, 128), F32),
            pltpu.VMEM((queries, n * kept), BF16),
            pltpu.VMEM((queries, n * kept), BF16),
            pltpu.VMEM((queries, queries), F32),
            pltpu.VMEM((n, cols, kept), F32),
            pltpu.VMEM((head, kept), F32),
            dma((2,)),
            dma((HALVES,)),
            dma((HALVES,)),
            dma((HALVES,)),
            dma((HALVES,)),
            dma((2, n)),
            dma((2, n)),
            dma,
            dma,
            dma((HALVES,)),
            dma((HALVES,)),
            dma((HALVES,)),
            dma((HALVES,)),
            dma,
            dma,
        ],
        compiler_params=pltpu.CompilerParams(
            collective_id=0, has_side_effects=True, vmem_limit_bytes=56 * 1024 * 1024
        ),
    )(cache_keys, cache_values, query_pool, kept_index, ref_index)


def solution(mesh):
    placed = (
        P("rep", "ctx", None),
        P("rep", "ctx", None),
        P("rep", "ctx", None),
        P("rep", "ctx"),
        P("rep", None),
    )
    return jax.shard_map(
        local, mesh=mesh, in_specs=placed, out_specs=P("rep", "ctx", None), check_vma=False
    )
```

time: 826 us -> 92.3 us (0.11)
  the two profiles are of different devices: /device:TPU:2 before, /device:TPU:4 now
where the time goes in v1:
time: 92.3 us; the launch traced here: 92.1 us
  Pallas kernels  90.5 us (98%)
  local copies, waits for them, and re-layouts  1.57 us (2%)
    pallas_call x1, Pallas kernels, local(): pl.pallas_call(functools.partial(kernel, n), out_shape=jax.ShapeDtypeStru...  90.5 us

profile of v1, /device:TPU:4, one launch (start us, length us, event | category | flops | bytes accessed | tf_op | source)
XLA Modules:
  0.0 92.1 jit_solution(15738935817985083322)
XLA Ops:
  0.0 90.5 %shard_map.55 = f32[1,256,128]{2,1,0:T(8,128)} custom-call(bf16[1,4096,128]{2,1,0:T(8,128)(2,1)} %keys_hbm.1, bf16[1,4096,128]{2,1,0:T(8,128)(2,1)} %vals_hbm.1, bf16[1,256,128]{2,1,0:T(8,128)(2,1)} %pool_ref.1, s32[1,256]{1,0:T(1,128)} %kept_ref.1, s32[1,512]{1,0:T(1,128)} %ref_ref.1), custom_call_target="tpu_custom_call" | custom-call | tf_op jit(solution)/shard_map/pallas_call | solution.py:352
  90.5 1.6 %copy.7 = f32[1,256,128]{2,1,0:T(8,128)} copy(f32[1,256,128]{2,1,0:T(8,128)} %shard_map.55) | data formatting | bytes 262144

commit v2 on v1

v2 whole, which is shorter than its diff:
```python
import functools

import jax
import jax.numpy as jnp
from jax import lax
from jax.experimental import pallas as pl
from jax.experimental.pallas import tpu as pltpu
from jax.sharding import PartitionSpec as P

ITERS = 3
HALVES = 2
OWNERS = 2
NEAR = 4
F32 = jnp.float32
BF16 = jnp.bfloat16
MESH = pl.DeviceIdType.MESH


def nt(a, b):
    return lax.dot_general(a, b, (((1,), (1,)), ((), ())), preferred_element_type=F32)


def nn(a, b):
    return lax.dot_general(a, b, (((1,), (0,)), ((), ())), preferred_element_type=F32)


def split(x):
    high = x.astype(BF16)
    return high, (x - high.astype(F32)).astype(BF16)


def kernel(
    n, keys_hbm, vals_hbm, pool_ref, kept_ref, ref_ref, out_ref,
    keys, vals, vals_t, q_part, q_recv, q_blk, q_all, kk_own, kk, v_t, v_recv,
    s_buf, p_t, stats, p_near, stats_near, p_sum, stats_sum, p_recv, stats_recv, a_buf, top_buf, a_high, a_low, gram, low_sums, res, fin,
    load_sem, q_send, q_got, g_send, g_got, kept_send, kept_got, v_send, v_got,
    p_send, p_got, st_send, st_got, ps_send, ps_got, sts_send, sts_got, f_send, f_got,
):
    me = lax.axis_index("ctx")
    rows, head = keys.shape
    kept = kk.shape[1]
    queries = q_all.shape[0]
    half = queries // HALVES
    blk = half // n
    cols = head // OWNERS
    apart = n // OWNERS
    scale = 1.0 / head**0.5
    ridge = 0.3 * queries / ((kept * n) * (kept * n))

    def peer(d):
        return {"ctx": lax.rem(me + d, n)}

    core = lax.rem(lax.axis_index("rep"), 2)
    offset = core * (apart // 2)
    place = lax.rem(me - offset + n, apart)
    owner = place == 0
    seat = lax.rem(place + NEAR - 1 - 2 * core, NEAR)

    def owned(ahead):
        first = lax.rem(me - place + ahead * apart - offset + n, n) // apart * cols
        return pl.ds(pl.multiple_of(first, cols), cols)

    def to_owners(send, keep):
        for ahead in reversed(range(OWNERS)):
            if ahead > 0:
                for copy in send(ahead, ahead * apart - place + n, lax.rem(place - ahead * apart + n, n)):
                    copy.start()
            else:

                @pl.when(place > 0)
                def _():
                    for copy in send(0, n - place, place):
                        copy.start()

                @pl.when(owner)
                def _():
                    keep()

    def sent_to_owners(send):
        for ahead in range(1, OWNERS):
            for copy in send(ahead, ahead * apart - place + n, lax.rem(place - ahead * apart + n, n)):
                copy.wait_send()

        @pl.when(place > 0)
        def _():
            for copy in send(0, n - place, place):
                copy.wait_send()

    def far_first(i):
        return n // 2 + (1 - 2 * (i % 2)) * ((i + 1) // 2)

    def sends(make):
        def body(i, carry):
            make(far_first(i)).start()
            return carry

        lax.fori_loop(0, n - 1, body, 0)

    def remote(src, dst, send, got, d):
        return pltpu.make_async_remote_copy(
            src_ref=src, dst_ref=dst, send_sem=send, recv_sem=got, device_id=peer(d), device_id_type=MESH
        )

    barrier = pltpu.get_barrier_semaphore()

    def greet(d, carry):
        pl.semaphore_signal(barrier, inc=1, device_id=peer(d), device_id_type=MESH)
        return carry

    lax.fori_loop(1, n, greet, 0)

    load_keys = pltpu.make_async_copy(keys_hbm.at[0], keys, load_sem.at[0])
    load_vals = pltpu.make_async_copy(vals_hbm.at[0], vals, load_sem.at[1])
    load_keys.start()
    load_vals.start()

    wanted = ref_ref[...] - me * pool_ref.shape[1]
    hit = lax.broadcasted_iota(jnp.int32, (pool_ref.shape[1], queries), 0) == wanted
    hit_t = jnp.where(hit, 1.0, 0.0).astype(F32).T.astype(BF16)
    q_part[...] = nn(hit_t, pool_ref[0]).astype(BF16)

    local = kept_ref[...] - me * rows
    local_col = jnp.broadcast_to(local, (128, kept)).T
    step = 512

    def chosen(i):
        base = lax.broadcasted_iota(jnp.int32, (kept, 128), 1) + i * step
        return jnp.concatenate(
            [jnp.where(local_col == base + 128 * j, 1.0, 0.0).astype(BF16) for j in range(step // 128)], axis=1
        )

    load_keys.wait()

    def pick_keys(i, carry):
        return carry + nn(chosen(i), keys[pl.ds(pl.multiple_of(i * step, step), step), :])

    kk_own[...] = lax.fori_loop(0, rows // step, pick_keys, jnp.zeros((kept, head), F32)).astype(BF16)

    def send_kept(ahead, d, slot):
        return (remote(kk_own, kk.at[slot], kept_send.at[ahead], kept_got.at[slot], d),)

    def keep_kept():
        kk[0] = kk_own[...]

    def send_vals(ahead, d, slot):
        return (remote(v_t.at[owned(ahead)], v_recv.at[slot], v_send.at[ahead], v_got, d),)

    def keep_vals():
        v_recv[0] = v_t[owned(0), :]

    pl.semaphore_wait(barrier, n - 1)

    for h in range(HALVES):

        def send_share(d, h=h):
            own = pl.ds(pl.multiple_of(h * half + lax.rem(me + d, n) * blk, blk), blk)
            return remote(q_part.at[own], q_recv.at[h, d], q_send.at[h], q_got.at[h], d)

        sends(send_share)
        mine = pl.ds(pl.multiple_of(h * half + me * blk, blk), blk)
        q_recv[h, 0] = q_part[mine, :]


    load_vals.wait()

    def pick_vals(i, carry):
        at = pl.ds(pl.multiple_of(i * step, step), step)
        vals_t[:, at] = vals[at, :].astype(F32).T.astype(BF16)
        return carry + nn(chosen(i), vals[at, :])

    kept_vals = lax.fori_loop(0, rows // step, pick_vals, jnp.zeros((kept, head), F32))
    v_t[...] = kept_vals.T.astype(BF16)

    for h in range(HALVES):
        got = q_recv.at[h, pl.ds(1, n - 1)]
        pltpu.make_async_copy(got, got, q_got.at[h]).wait()
        total = q_recv[h, 0].astype(F32)
        for d in range(1, n):
            total = total + q_recv[h, d].astype(F32)
        q_blk[h] = total.astype(BF16)
        mine = pl.ds(pl.multiple_of(h * half + me * blk, blk), blk)

        def send_block(d, h=h, mine=mine):
            return remote(q_blk.at[h], q_all.at[mine], g_send.at[h], g_got.at[h], d)

        sends(send_block)
        q_all[mine, :] = q_blk[h]


    def near_target(h, d, slot):
        return (
            remote(stats.at[h], stats_near.at[h, slot], st_send.at[h], st_got.at[h, slot], d),
            remote(p_t.at[h], p_near.at[h, slot], p_send.at[h], p_got.at[h, slot], d),
        )

    for h in range(HALVES):
        got = q_all.at[pl.ds(0, (n - 1) * blk)]
        pltpu.make_async_copy(got, got, g_got.at[h]).wait()
        if h == 0:
            to_owners(send_kept, keep_kept)
        if h == 1:
            to_owners(send_vals, keep_vals)
        q_half = q_all[h * half : (h + 1) * half, :]

        def score(i, top):
            at = pl.ds(pl.multiple_of(i * step, step), step)
            s = nt(keys[at, :], q_half) * scale
            s_buf[at, :] = s
            return jnp.maximum(top, jnp.max(s.reshape(step // 8, 8, half), axis=0))

        top = lax.fori_loop(0, rows // step, score, jnp.full((8, half), -jnp.inf, F32))
        top = jnp.max(top, axis=0, keepdims=True)

        def weigh(i, carry):
            at = pl.ds(pl.multiple_of(i * step, step), step)
            e = jnp.exp(s_buf[at, :] - top)
            total = carry[0] + jnp.sum(e.reshape(step // 8, 8, half), axis=0)
            return total, carry[1] + nn(vals_t[:, at], e.astype(BF16))

        total, weighted = lax.fori_loop(
            0, rows // step, weigh, (jnp.zeros((8, half), F32), jnp.zeros((head, half), F32))
        )
        total = jnp.sum(total, axis=0, keepdims=True)
        p_t[h] = weighted
        for j in range(half // 128):
            stats[h, j : j + 1, :] = top[:, j * 128 : (j + 1) * 128]
            stats[h, 2 + j : 3 + j, :] = total[:, j * 128 : (j + 1) * 128]

        for where, d, slot in ((1, n - 1, 1), (3, 1, 2), (2, n - 2 if h == 0 else 2, 3)):

            @pl.when(seat == where)
            def _(h=h, d=d, slot=slot):
                for copy in near_target(h, d, slot):
                    copy.start()

    def columns_at(d):
        return pl.ds(pl.multiple_of(lax.rem(me + d - offset + 2 * n, n) // apart * cols, cols), cols)

    below, above = (n - place, place // NEAR), (apart - place, place // NEAR + 2)

    def far_target(h, route):
        d, slot = route
        return (
            remote(stats_sum.at[h], stats_recv.at[h, slot], sts_send.at[h, slot], sts_got.at[h, slot], d),
            remote(p_sum.at[h, columns_at(d)], p_recv.at[h, slot], ps_send.at[h, slot], ps_got.at[h, slot], d),
        )

    def merge_near(h):
        for slot in (1, 2, 3):
            for copy in near_target(h, 1, slot):
                copy.wait_recv()
        for j in range(half // 128):
            lanes = slice(j * 128, (j + 1) * 128)
            tops = [stats[h, j : j + 1, :]] + [stats_near[h, slot, j : j + 1, :] for slot in (1, 2, 3)]
            best = functools.reduce(jnp.maximum, tops)
            factors = [jnp.exp(top - best) for top in tops]
            total = factors[0] * stats[h, 2 + j : 3 + j, :]
            weighted = factors[0] * p_t[h, :, lanes]
            for slot in (1, 2, 3):
                total = total + factors[slot] * stats_near[h, slot, 2 + j : 3 + j, :]
                weighted = weighted + factors[slot] * p_near[h, slot, :, lanes]
            stats_sum[h, j : j + 1, :] = best
            stats_sum[h, 2 + j : 3 + j, :] = total
            p_sum[h, :, lanes] = weighted

    @pl.when(seat == 0)
    def _():
        for h in range(HALVES):
            merge_near(h)
            for route in (below, above):
                for copy in far_target(h, route):
                    copy.start()

    @pl.when(owner)
    def _():
        q_now = q_all[...]
        top_buf[...] = jnp.full(top_buf.shape, -jnp.inf, F32)

        def kept_scores(slot):
            s = nt(q_now, kk[slot]) * scale
            a_buf[:, pl.ds(pl.multiple_of(slot * kept, kept), kept)] = s
            best = top_buf[...]
            for j in range(kept // 128):
                best = jnp.maximum(best, s[:, j * 128 : (j + 1) * 128])
            top_buf[...] = best

        def kept_scores_body(slot, carry):
            kept_scores(slot)
            return carry

        kept_scores(0)

        def arrived(i, carry):
            slot = i + 1 + (i + 1) // 8 * (n + 5 - 2 * i)
            pltpu.make_async_copy(kk.at[slot], kk.at[slot], kept_got.at[slot]).wait()
            kept_scores(slot)
            return carry

        lax.fori_loop(0, n - 1, arrived, 0)
        best = jnp.max(top_buf[...], axis=1, keepdims=True)
        top_buf[...] = jnp.broadcast_to(best, top_buf.shape)

        def kept_weights(i, carry):
            at = pl.ds(pl.multiple_of(i * 128, 128), 128)
            high, low = split(jnp.exp(a_buf[:, at] - top_buf[...]))
            a_high[:queries, at] = high
            a_low[:, at] = low + low
            return carry

        lax.fori_loop(0, n * kept // 128, kept_weights, 0)

        got = v_recv.at[pl.ds(1, n - 1)]
        pltpu.make_async_copy(got, got, v_got).wait()
        for d in range(n):
            a_high[queries : queries + cols, d * kept : (d + 1) * kept] = v_recv[d]
        a_high[queries + cols :, :] = jnp.ones((16, n * kept), BF16)
        def products(i, carry):
            at = pl.ds(pl.multiple_of(i * 256, 256), 256)
            gram[:, at] = nt(a_high[...], a_high[at, :])
            low_sums[:, at] = nt(a_high[...], a_low[at, :])
            return carry

        lax.fori_loop(0, queries // 256, products, 0)
        sums = gram[queries:, :] + 0.5 * low_sums[queries:, :]
        inverse = 1.0 / sums[cols : cols + 1, :]
        fitted_now = sums[:cols, :] * inverse
        once = gram[:queries, :] + low_sums[:queries, :]
        gram_high, gram_low = split(0.5 * (once + once.T))

        pieces = []
        for h in range(HALVES):
            for slot in range(4):
                for copy in far_target(h, (NEAR, slot)):
                    copy.wait_recv()
            for j in range(half // 128):
                tops = stats_recv[h, :, j : j + 1, :]
                totals = stats_recv[h, :, 2 + j : 3 + j, :]
                factor = jnp.exp(tops - jnp.max(tops, axis=0, keepdims=True))
                weighted = jnp.sum(factor * p_recv[h, :, :, j * 128 : (j + 1) * 128], axis=0)
                pieces.append(weighted / jnp.sum(factor * totals, axis=0))
        target = jnp.concatenate(pieces, axis=1)

        def apply(x):
            high, low = split(x * inverse)
            both = nn(jnp.concatenate([high, low], axis=0), gram_high)
            return (both[:cols] + both[cols:] + nn(high, gram_low)) * inverse

        def dots(a, b):
            return jnp.sum(a * b, axis=1, keepdims=True)

        y = target - fitted_now
        image_y = apply(y)
        norm_now = dots(y, image_y)
        u, image = y, image_y
        answer = jnp.zeros_like(y)
        for it in range(ITERS):
            curve = dots(image, image) + ridge * dots(u, image)
            alpha = norm_now / curve
            answer = answer + alpha * u
            if it == ITERS - 1:
                break
            y = y - alpha * (image + ridge * u)
            image_y = apply(y)
            norm_next = dots(y, image_y)
            beta = norm_next / norm_now
            u = y + beta * u
            image = image_y + beta * image
            norm_now = norm_next

        high, low = split(answer * inverse)
        both_ways = jnp.concatenate([high, low], axis=0)

        def result(slot):
            at = pl.ds(pl.multiple_of(slot * kept, kept), kept)
            both = nn(both_ways, a_high[:queries, at])
            return v_recv[slot].astype(F32) + both[:cols] + both[cols:] + 0.5 * nn(high, a_low[:, at])

        def give(i, carry):
            d = far_first(i)
            res[d] = result(d)
            remote(res.at[d], fin.at[owned(0)], f_send, f_got, d).start()
            return carry

        lax.fori_loop(0, n - 1, give, 0)
        fin[owned(0), :] = result(0)

    def drain(ref, sem):
        pltpu.make_async_copy(ref, ref, sem).wait()

    for h in range(HALVES):
        drain(q_recv.at[h, pl.ds(1, n - 1)], q_send.at[h])
        drain(q_all.at[pl.ds(0, (n - 1) * blk)], g_send.at[h])
    sent_to_owners(send_vals)
    sent_to_owners(send_kept)

    @pl.when(owner)
    def _():
        drain(res.at[pl.ds(1, n - 1)], f_send)
        drain(fin.at[pl.ds(0, head - cols)], f_got)

    @pl.when(seat == 0)
    def _():
        for h in range(HALVES):
            for route in (below, above):
                for copy in far_target(h, route):
                    copy.wait_send()

    @pl.when(seat > 0)
    def _():
        for h in range(HALVES):
            for copy in near_target(h, 1, 1):
                copy.wait_send()

    @pl.when(place > 0)
    def _():
        drain(fin, f_got)

    out_ref[0] = fin[...].T


def local(cache_keys, cache_values, query_pool, kept_index, ref_index):
    n = lax.axis_size("ctx")
    rows, head = cache_keys.shape[1:]
    kept = kept_index.shape[1]
    queries = ref_index.shape[1]
    half = queries // HALVES
    blk = half // n
    cols = head // OWNERS
    vmem = pl.BlockSpec(memory_space=pltpu.VMEM)
    hbm = pl.BlockSpec(memory_space=pl.ANY)
    dma = pltpu.SemaphoreType.DMA
    return pl.pallas_call(
        functools.partial(kernel, n),
        out_shape=jax.ShapeDtypeStruct((1, kept, head), F32),
        in_specs=[hbm, hbm, vmem, vmem, vmem],
        out_specs=vmem,
        scratch_shapes=[
            pltpu.VMEM((rows, head), BF16),
            pltpu.VMEM((rows, head), BF16),
            pltpu.VMEM((head, rows), BF16),
            pltpu.VMEM((queries, head), BF16),
            pltpu.VMEM((HALVES, n, blk, head), BF16),
            pltpu.VMEM((HALVES, blk, head), BF16),
            pltpu.VMEM((queries, head), BF16),
            pltpu.VMEM((kept, head), BF16),
            pltpu.VMEM((n, kept, head), BF16),
            pltpu.VMEM((head, kept), BF16),
            pltpu.VMEM((n, cols, kept), BF16),
            pltpu.VMEM((rows, half), F32),
            pltpu.VMEM((HALVES, head, half), F32),
            pltpu.VMEM((HALVES, 4, 128), F32),
            pltpu.VMEM((HALVES, 4, head, half), F32),
            pltpu.VMEM((HALVES, 4, 4, 128), F32),
            pltpu.VMEM((HALVES, head, half), F32),
            pltpu.VMEM((HALVES, 4, 128), F32),
            pltpu.VMEM((HALVES, 4, cols, half), F32),
            pltpu.VMEM((HALVES, 4, 4, 128), F32),
            pltpu.VMEM((queries, n * kept), F32),
            pltpu.VMEM((queries, 128), F32),
            pltpu.VMEM((queries + cols + 16, n * kept), BF16),
            pltpu.VMEM((queries, n * kept), BF16),
            pltpu.VMEM((queries + cols + 16, queries), F32),
            pltpu.VMEM((queries + cols + 16, queries), F32),
            pltpu.VMEM((n, cols, kept), F32),
            pltpu.VMEM((head, kept), F32),
            dma((2,)),
            dma((HALVES,)),
            dma((HALVES,)),
            dma((HALVES,)),
            dma((HALVES,)),
            dma((OWNERS,)),
            dma((n,)),
            dma((OWNERS,)),
            dma,
            dma((HALVES,)),
            dma((HALVES, 4)),
            dma((HALVES,)),
            dma((HALVES, 4)),
            dma((HALVES, 4)),
            dma((HALVES, 4)),
            dma((HALVES, 4)),
            dma((HALVES, 4)),
            dma,
            dma,
        ],
        compiler_params=pltpu.CompilerParams(
            collective_id=0, has_side_effects=True, vmem_limit_bytes=56 * 1024 * 1024
        ),
    )(cache_keys, cache_values, query_pool, kept_index, ref_index)


def solution(mesh):
    placed = (
        P("rep", "ctx", None),
        P("rep", "ctx", None),
        P("rep", "ctx", None),
        P("rep", "ctx"),
        P("rep", None),
    )
    return jax.shard_map(
        local, mesh=mesh, in_specs=placed, out_specs=P("rep", "ctx", None), check_vma=False
    )
```

time: 92.3 us -> 68.9 us (0.75)
  the two profiles are of different devices: /device:TPU:4 before, /device:TPU:2 now
where the time goes in v2:
time: 68.9 us; the launch traced here: 68.7 us
  Pallas kernels  67.1 us (97%)
  local copies, waits for them, and re-layouts  1.57 us (2%)
    pallas_call x1, Pallas kernels, local(): pl.pallas_call(functools.partial(kernel, n), out_shape=jax.ShapeDtypeStru...  67.1 us
    unnamed x1, local copies, waits for them, and re-layouts  1.57 us

profile of v2, /device:TPU:2, one launch (start us, length us, event | category | flops | bytes accessed | tf_op | source)
XLA Modules:
  0.0 68.7 jit_solution(8526118918925926561)
XLA Ops:
  0.0 67.1 %shard_map.55 = f32[1,256,128]{2,1,0:T(8,128)} custom-call(bf16[1,4096,128]{2,1,0:T(8,128)(2,1)} %keys_hbm.1, bf16[1,4096,128]{2,1,0:T(8,128)(2,1)} %vals_hbm.1, bf16[1,256,128]{2,1,0:T(8,128)(2,1)} %pool_ref.1, s32[1,256]{1,0:T(1,128)} %kept_ref.1, s32[1,512]{1,0:T(1,128)} %ref_ref.1), custom_call_target="tpu_custom_call" | custom-call | tf_op jit(solution)/shard_map/pallas_call | solution.py:432
  67.1 1.6 %copy.7 = f32[1,256,128]{2,1,0:T(8,128)} copy(f32[1,256,128]{2,1,0:T(8,128)} %shard_map.55) | data formatting | bytes 262144

commit v3 on v2

--- a/solution.py
+++ b/solution.py
@@ -30,11 +30,12 @@
 
 
 def kernel(
-    n, keys_hbm, vals_hbm, pool_ref, kept_ref, ref_ref, out_ref,
+    n, keys_hbm, vals_hbm, pool_hbm, kept_hbm, ref_hbm, out_ref,
+    pool_ref, kept_ref, ref_ref,
     keys, vals, vals_t, q_part, q_recv, q_blk, q_all, kk_own, kk, v_t, v_recv,
-    s_buf, p_t, stats, p_near, stats_near, p_sum, stats_sum, p_recv, stats_recv, a_buf, top_buf, a_high, a_low, gram, low_sums, res, fin,
+    s_buf, p_t, stats, p_near, stats_near, p_sum, stats_sum, p_recv, stats_recv, a_buf, top_buf, a_both, rows_v, gram, res, fin, units, fin_units, turned, vals_own,
     load_sem, q_send, q_got, g_send, g_got, kept_send, kept_got, v_send, v_got,
-    p_send, p_got, st_send, st_got, ps_send, ps_got, sts_send, sts_got, f_send, f_got,
+    p_send, p_got, st_send, st_got, ps_send, ps_got, sts_send, sts_got, f_send, f_got, u_send, u_got,
 ):
     me = lax.axis_index("ctx")
     rows, head = keys.shape
@@ -56,6 +57,8 @@
     owner = place == 0
     seat = lax.rem(place + NEAR - 1 - 2 * core, NEAR)
 
+    column_block = lax.rem(me - place - offset + n, n) // apart
+
     def owned(ahead):
         first = lax.rem(me - place + ahead * apart - offset + n, n) // apart * cols
         return pl.ds(pl.multiple_of(first, cols), cols)
@@ -109,11 +112,19 @@
 
     lax.fori_loop(1, n, greet, 0)
 
+    loads = [
+        pltpu.make_async_copy(src, dst, load_sem.at[2 + i])
+        for i, (src, dst) in enumerate(((ref_hbm, ref_ref), (pool_hbm, pool_ref), (kept_hbm, kept_ref)))
+    ]
+    for load in loads:
+        load.start()
     load_keys = pltpu.make_async_copy(keys_hbm.at[0], keys, load_sem.at[0])
     load_vals = pltpu.make_async_copy(vals_hbm.at[0], vals, load_sem.at[1])
     load_keys.start()
     load_vals.start()
 
+    for load in loads:
+        load.wait()
     wanted = ref_ref[...] - me * pool_ref.shape[1]
     hit = lax.broadcasted_iota(jnp.int32, (pool_ref.shape[1], queries), 0) == wanted
     hit_t = jnp.where(hit, 1.0, 0.0).astype(F32).T.astype(BF16)
@@ -169,6 +180,7 @@
         return carry + nn(chosen(i), vals[at, :])
 
     kept_vals = lax.fori_loop(0, rows // step, pick_vals, jnp.zeros((kept, head), F32))
+    vals_own[...] = kept_vals
     v_t[...] = kept_vals.T.astype(BF16)
 
     for h in range(HALVES):
@@ -187,51 +199,62 @@
         q_all[mine, :] = q_blk[h]
 
 
+    @pl.when(core == 0)
+    def _():
+        to_owners(send_kept, keep_kept)
+
+
     def near_target(h, d, slot):
         return (
             remote(stats.at[h], stats_near.at[h, slot], st_send.at[h], st_got.at[h, slot], d),
             remote(p_t.at[h], p_near.at[h, slot], p_send.at[h], p_got.at[h, slot], d),
         )
 
-    for h in range(HALVES):
+    span = min(rows, 2048)
+
+    def attention(h, carry):
         got = q_all.at[pl.ds(0, (n - 1) * blk)]
         pltpu.make_async_copy(got, got, g_got.at[h]).wait()
-        if h == 0:
+
+        @pl.when((h == 0) & (core == 1))
+        def _():
             to_owners(send_kept, keep_kept)
-        if h == 1:
-            to_owners(send_vals, keep_vals)
-        q_half = q_all[h * half : (h + 1) * half, :]
+
+        q_turned = q_all[pl.ds(pl.multiple_of(h * half, half), half), :].astype(F32).T.astype(BF16)
 
         def score(i, top):
-            at = pl.ds(pl.multiple_of(i * step, step), step)
-            s = nt(keys[at, :], q_half) * scale
+            at = pl.ds(pl.multiple_of(i * span, span), span)
+            s = nn(keys[at, :], q_turned) * scale
             s_buf[at, :] = s
-            return jnp.maximum(top, jnp.max(s.reshape(step // 8, 8, half), axis=0))
-
-        top = lax.fori_loop(0, rows // step, score, jnp.full((8, half), -jnp.inf, F32))
+            return jnp.maximum(top, jnp.max(s.reshape(span // 8, 8, half), axis=0))
+
+        top = lax.fori_loop(0, rows // span, score, jnp.full((8, half), -jnp.inf, F32))
         top = jnp.max(top, axis=0, keepdims=True)
 
         def weigh(i, carry):
-            at = pl.ds(pl.multiple_of(i * step, step), step)
+            at = pl.ds(pl.multiple_of(i * span, span), span)
             e = jnp.exp(s_buf[at, :] - top)
-            total = carry[0] + jnp.sum(e.reshape(step // 8, 8, half), axis=0)
+            total = carry[0] + jnp.sum(e.reshape(span // 8, 8, half), axis=0)
             return total, carry[1] + nn(vals_t[:, at], e.astype(BF16))
 
         total, weighted = lax.fori_loop(
-            0, rows // step, weigh, (jnp.zeros((8, half), F32), jnp.zeros((head, half), F32))
+            0, rows // span, weigh, (jnp.zeros((8, half), F32), jnp.zeros((head, half), F32))
         )
         total = jnp.sum(total, axis=0, keepdims=True)
         p_t[h] = weighted
-        for j in range(half // 128):
-            stats[h, j : j + 1, :] = top[:, j * 128 : (j + 1) * 128]
-            stats[h, 2 + j : 3 + j, :] = total[:, j * 128 : (j + 1) * 128]
-
-        for where, d, slot in ((1, n - 1, 1), (3, 1, 2), (2, n - 2 if h == 0 else 2, 3)):
+        lanes = [slice(j * 128, (j + 1) * 128) for j in range(half // 128)]
+        stats[h] = jnp.concatenate([top[:, at] for at in lanes] + [total[:, at] for at in lanes], axis=0)
+        for where, d, slot in ((1, n - 1, 1), (3, 1, 2), (2, n - 2 + 4 * h, 3)):
 
             @pl.when(seat == where)
-            def _(h=h, d=d, slot=slot):
+            def _(d=d, slot=slot):
                 for copy in near_target(h, d, slot):
                     copy.start()
+
+        return carry
+
+    lax.fori_loop(0, HALVES, attention, 0)
+    to_owners(send_vals, keep_vals)
 
     def columns_at(d):
         return pl.ds(pl.multiple_of(lax.rem(me + d - offset + 2 * n, n) // apart * cols, cols), cols)
@@ -276,56 +299,62 @@
         q_now = q_all[...]
         top_buf[...] = jnp.full(top_buf.shape, -jnp.inf, F32)
 
-        def kept_scores(slot):
-            s = nt(q_now, kk[slot]) * scale
-            a_buf[:, pl.ds(pl.multiple_of(slot * kept, kept), kept)] = s
+        def kept_scores(first, count):
+            wide = pl.ds(pl.multiple_of(first * kept, kept), count * kept)
+            s = nt(q_now, kk[pl.ds(first, count)].reshape(count * kept, head)) * scale
+            a_buf[:, wide] = s
             best = top_buf[...]
-            for j in range(kept // 128):
+            for j in range(count * kept // 128):
                 best = jnp.maximum(best, s[:, j * 128 : (j + 1) * 128])
             top_buf[...] = best
 
-        def kept_scores_body(slot, carry):
-            kept_scores(slot)
+        def arrived(i, carry):
+            first = i // 2 * NEAR + i % 2 * (n - NEAR - i // 2 * 2 * NEAR)
+            for j in range(NEAR):
+
+                @pl.when(first + j > 0)
+                def _(j=j):
+                    slot = kk.at[first + j]
+                    pltpu.make_async_copy(slot, slot, kept_got.at[first + j]).wait()
+
+            kept_scores(first, NEAR)
             return carry
 
-        kept_scores(0)
-
-        def arrived(i, carry):
-            slot = i + 1 + (i + 1) // 8 * (n + 5 - 2 * i)
-            pltpu.make_async_copy(kk.at[slot], kk.at[slot], kept_got.at[slot]).wait()
-            kept_scores(slot)
-            return carry
-
-        lax.fori_loop(0, n - 1, arrived, 0)
+        lax.fori_loop(0, n // NEAR, arrived, 0)
         best = jnp.max(top_buf[...], axis=1, keepdims=True)
         top_buf[...] = jnp.broadcast_to(best, top_buf.shape)
 
         def kept_weights(i, carry):
-            at = pl.ds(pl.multiple_of(i * 128, 128), 128)
-            high, low = split(jnp.exp(a_buf[:, at] - top_buf[...]))
-            a_high[:queries, at] = high
-            a_low[:, at] = low + low
+            at = pl.ds(pl.multiple_of(i * 1024, 1024), 1024)
+            for r in range(0, queries, 16):
+                some = slice(r, r + 16)
+                top = jnp.concatenate([top_buf[some, :]] * 8, axis=1)
+                high, low = split(jnp.exp(a_buf[some, at] - top))
+                a_both[0, some, at] = high
+                a_both[1, some, at] = low + low
             return carry
 
-        lax.fori_loop(0, n * kept // 128, kept_weights, 0)
+        lax.fori_loop(0, n * kept // 1024, kept_weights, 0)
+
+        def products(i, carry):
+            which = i // (queries // 256)
+            at = pl.ds(pl.multiple_of(i % (queries // 256) * 256, 256), 256)
+            gram[which, :, at] = nt(a_both[0], a_both[which, at, :])
+            return carry
+
+        lax.fori_loop(0, 2 * (queries // 256), products, 0)
+        once = gram[0] + gram[1]
+        gram_high, gram_low = split(0.5 * (once + once.T))
 
         got = v_recv.at[pl.ds(1, n - 1)]
         pltpu.make_async_copy(got, got, v_got).wait()
         for d in range(n):
-            a_high[queries : queries + cols, d * kept : (d + 1) * kept] = v_recv[d]
-        a_high[queries + cols :, :] = jnp.ones((16, n * kept), BF16)
-        def products(i, carry):
-            at = pl.ds(pl.multiple_of(i * 256, 256), 256)
-            gram[:, at] = nt(a_high[...], a_high[at, :])
-            low_sums[:, at] = nt(a_high[...], a_low[at, :])
-            return carry
-
-        lax.fori_loop(0, queries // 256, products, 0)
-        sums = gram[queries:, :] + 0.5 * low_sums[queries:, :]
+            rows_v[:cols, d * kept : (d + 1) * kept] = v_recv[d]
+        rows_v[cols:, :] = jnp.ones((16, n * kept), BF16)
+        rows_aug = rows_v[...]
+        sums = nt(rows_aug, a_both[0]) + 0.5 * nt(rows_aug, a_both[1])
         inverse = 1.0 / sums[cols : cols + 1, :]
         fitted_now = sums[:cols, :] * inverse
-        once = gram[:queries, :] + low_sums[:queries, :]
-        gram_high, gram_low = split(0.5 * (once + once.T))
 
         pieces = []
         for h in range(HALVES):
@@ -370,19 +399,34 @@
         high, low = split(answer * inverse)
         both_ways = jnp.concatenate([high, low], axis=0)
 
-        def result(slot):
-            at = pl.ds(pl.multiple_of(slot * kept, kept), kept)
-            both = nn(both_ways, a_high[:queries, at])
-            return v_recv[slot].astype(F32) + both[:cols] + both[cols:] + 0.5 * nn(high, a_low[:, at])
-
-        def give(i, carry):
-            d = far_first(i)
-            res[d] = result(d)
-            remote(res.at[d], fin.at[owned(0)], f_send, f_got, d).start()
+        def give(first):
+            at = pl.ds(pl.multiple_of(first * kept, 2 * kept), 2 * kept)
+            both = nn(both_ways, a_both[0, :queries, at])
+            change = both[:cols] + both[cols:] + 0.5 * nn(high, a_both[1, :queries, at])
+            largest = jnp.max(jnp.abs(change), axis=0, keepdims=True)
+            factor = jnp.where(largest > 1e-30, 32767.0 / jnp.maximum(largest, 1e-30), 0.0)
+            codes = jnp.round(change * factor).astype(jnp.int32).astype(jnp.int16)
+            unit = largest * (1.0 / 32767.0)
+            for j in range(2):
+                d = first + j
+                res[d] = codes[:, j * kept : (j + 1) * kept]
+                units[d] = jnp.concatenate(
+                    [unit[:, j * kept + k * 128 : j * kept + (k + 1) * 128] for k in range(kept // 128)], axis=0
+                )
+
+                @pl.when(d > 0)
+                def _(d=d):
+                    remote(res.at[d], fin.at[owned(0)], f_send, f_got, d).start()
+                    remote(units.at[d], fin_units.at[column_block], u_send, u_got, d).start()
+
+        def give_pairs(i, carry):
+            give(n // 2 + 2 * i)
+            give(n // 2 - 2 - 2 * i)
             return carry
 
-        lax.fori_loop(0, n - 1, give, 0)
-        fin[owned(0), :] = result(0)
+        lax.fori_loop(0, n // 4, give_pairs, 0)
+        fin[owned(0), :] = res[0]
+        fin_units[column_block] = units[0]
 
     def drain(ref, sem):
         pltpu.make_async_copy(ref, ref, sem).wait()
@@ -396,7 +440,9 @@
     @pl.when(owner)
     def _():
         drain(res.at[pl.ds(1, n - 1)], f_send)
+        drain(units.at[pl.ds(1, n - 1)], u_send)
         drain(fin.at[pl.ds(0, head - cols)], f_got)
+        drain(fin_units.at[pl.ds(0, OWNERS - 1)], u_got)
 
     @pl.when(seat == 0)
     def _():
@@ -414,14 +460,20 @@
     @pl.when(place > 0)
     def _():
         drain(fin, f_got)
-
-    out_ref[0] = fin[...].T
+        drain(fin_units, u_got)
+
+    for j in range(OWNERS):
+        at = slice(j * cols, (j + 1) * cols)
+        unit = jnp.concatenate([fin_units[j, k : k + 1, :] for k in range(kept // 128)], axis=1)
+        turned[at, :] = fin[at, :].astype(jnp.int32).astype(F32) * unit
+    out_ref[0] = vals_own[...] + turned[...].T
 
 
 def local(cache_keys, cache_values, query_pool, kept_index, ref_index):
     n = lax.axis_size("ctx")
     rows, head = cache_keys.shape[1:]
     kept = kept_index.shape[1]
+    pool = query_pool.shape[1]
     queries = ref_index.shape[1]
     half = queries // HALVES
     blk = half // n
@@ -432,9 +484,12 @@
     return pl.pallas_call(
         functools.partial(kernel, n),
         out_shape=jax.ShapeDtypeStruct((1, kept, head), F32),
-        in_specs=[hbm, hbm, vmem, vmem, vmem],
+        in_specs=[hbm] * 5,
         out_specs=vmem,
         scratch_shapes=[
+            pltpu.VMEM((1, pool, head), BF16),
+            pltpu.VMEM((1, kept), jnp.int32),
+            pltpu.VMEM((1, queries), jnp.int32),
             pltpu.VMEM((rows, head), BF16),
             pltpu.VMEM((rows, head), BF16),
             pltpu.VMEM((head, rows), BF16),
@@ -457,13 +512,16 @@
             pltpu.VMEM((HALVES, 4, 4, 128), F32),
             pltpu.VMEM((queries, n * kept), F32),
             pltpu.VMEM((queries, 128), F32),
-            pltpu.VMEM((queries + cols + 16, n * kept), BF16),
-            pltpu.VMEM((queries, n * kept), BF16),
-            pltpu.VMEM((queries + cols + 16, queries), F32),
-            pltpu.VMEM((queries + cols + 16, queries), F32),
-            pltpu.VMEM((n, cols, kept), F32),
+            pltpu.VMEM((2, queries, n * kept), BF16),
+            pltpu.VMEM((cols + 16, n * kept), BF16),
+            pltpu.VMEM((2, queries, queries), F32),
+            pltpu.VMEM((n, cols, kept), jnp.int16),
+            pltpu.VMEM((head, kept), jnp.int16),
+            pltpu.VMEM((n, kept // 128, 128), F32),
+            pltpu.VMEM((OWNERS, kept // 128, 128), F32),
             pltpu.VMEM((head, kept), F32),
-            dma((2,)),
+            pltpu.VMEM((kept, head), F32),
+            dma((5,)),
             dma((HALVES,)),
             dma((HALVES,)),
             dma((HALVES,)),
@@ -482,6 +540,8 @@
             dma((HALVES, 4)),
             dma,
             dma,
+            dma,
+            dma,
         ],
         compiler_params=pltpu.CompilerParams(
             collective_id=0, has_side_effects=True, vmem_limit_bytes=56 * 1024 * 1024

time: 68.9 us -> 64.5 us (0.936)
  the two profiles are of different devices: /device:TPU:2 before, /device:TPU:48 now
where the time goes in v3:
time: 64.5 us; the launch traced here: 64.3 us
  Pallas kernels  62.7 us (97%)
  local copies, waits for them, and re-layouts  1.57 us (2%)
    pallas_call x1, Pallas kernels, local(): pl.pallas_call(functools.partial(kernel, n), out_shape=jax.ShapeDtypeStru...  62.7 us
    unnamed x1, local copies, waits for them, and re-layouts  1.57 us

profile of v3, /device:TPU:48, one launch (start us, length us, event | category | flops | bytes accessed | tf_op | source)
XLA Modules:
  0.0 64.3 jit_solution(14464502391672062151)
XLA Ops:
  0.0 62.7 %shard_map.55 = f32[1,256,128]{2,1,0:T(8,128)} custom-call(bf16[1,4096,128]{2,1,0:T(8,128)(2,1)} %keys_hbm.1, bf16[1,4096,128]{2,1,0:T(8,128)(2,1)} %vals_hbm.1, bf16[1,256,128]{2,1,0:T(8,128)(2,1)} %pool_hbm.1, s32[1,256]{1,0:T(1,128)} %kept_hbm.1, s32[1,512]{1,0:T(1,128)} %ref_hbm.1), custom_call_target="tpu_custom_call" | custom-call | tf_op jit(solution)/shard_map/pallas_call | solution.py:484
  62.7 1.6 %copy.7 = f32[1,256,128]{2,1,0:T(8,128)} copy(f32[1,256,128]{2,1,0:T(8,128)} %shard_map.55) | data formatting | bytes 262144

commit v4 on v3

--- a/solution.py
+++ b/solution.py
@@ -33,7 +33,7 @@
     n, keys_hbm, vals_hbm, pool_hbm, kept_hbm, ref_hbm, out_ref,
     pool_ref, kept_ref, ref_ref,
     keys, vals, vals_t, q_part, q_recv, q_blk, q_all, kk_own, kk, v_t, v_recv,
-    s_buf, p_t, stats, p_near, stats_near, p_sum, stats_sum, p_recv, stats_recv, a_buf, top_buf, a_both, rows_v, gram, res, fin, units, fin_units, turned, vals_own,
+    s_buf, p_t, stats, p_near, stats_near, p_sum, stats_sum, p_recv, stats_recv, a_buf, top_buf, a_both, gram, res, fin, units, fin_units, turned, vals_own,
     load_sem, q_send, q_got, g_send, g_got, kept_send, kept_got, v_send, v_got,
     p_send, p_got, st_send, st_got, ps_send, ps_got, sts_send, sts_got, f_send, f_got, u_send, u_got,
 ):
@@ -220,6 +220,10 @@
         def _():
             to_owners(send_kept, keep_kept)
 
+        @pl.when(h == 1)
+        def _():
+            to_owners(send_vals, keep_vals)
+
         q_turned = q_all[pl.ds(pl.multiple_of(h * half, half), half), :].astype(F32).T.astype(BF16)
 
         def score(i, top):
@@ -254,7 +258,6 @@
         return carry
 
     lax.fori_loop(0, HALVES, attention, 0)
-    to_owners(send_vals, keep_vals)
 
     def columns_at(d):
         return pl.ds(pl.multiple_of(lax.rem(me + d - offset + 2 * n, n) // apart * cols, cols), cols)
@@ -336,25 +339,30 @@
 
         lax.fori_loop(0, n * kept // 1024, kept_weights, 0)
 
-        def products(i, carry):
-            which = i // (queries // 256)
-            at = pl.ds(pl.multiple_of(i % (queries // 256) * 256, 256), 256)
-            gram[which, :, at] = nt(a_both[0], a_both[which, at, :])
-            return carry
-
-        lax.fori_loop(0, 2 * (queries // 256), products, 0)
-        once = gram[0] + gram[1]
-        gram_high, gram_low = split(0.5 * (once + once.T))
+        wide = queries // 2
+        gram[0, :wide, :wide] = nt(a_both[0, :wide, :], a_both[0, :wide, :])
+        gram[0, wide:queries, :wide] = jnp.zeros((queries - wide, wide), F32)
+        right = nt(a_both[0, :queries, :], a_both[0, wide:queries, :])
+        gram[0, :wide, wide:] = right[:wide] + right[:wide]
+        gram[0, wide:queries, wide:] = right[wide:]
 
         got = v_recv.at[pl.ds(1, n - 1)]
         pltpu.make_async_copy(got, got, v_got).wait()
         for d in range(n):
-            rows_v[:cols, d * kept : (d + 1) * kept] = v_recv[d]
-        rows_v[cols:, :] = jnp.ones((16, n * kept), BF16)
-        rows_aug = rows_v[...]
-        sums = nt(rows_aug, a_both[0]) + 0.5 * nt(rows_aug, a_both[1])
+            a_both[0, queries : queries + cols, d * kept : (d + 1) * kept] = v_recv[d]
+        a_both[0, queries + cols :, :] = jnp.ones((16, n * kept), BF16)
+
+        def products(i, carry):
+            at = pl.ds(pl.multiple_of(i * wide, wide), wide)
+            gram[1, :, at] = nt(a_both[0], a_both[1, at, :])
+            return carry
+
+        lax.fori_loop(0, queries // wide, products, 0)
+        sums = nt(a_both[0, queries:, :], a_both[0, :queries, :]) + 0.5 * gram[1, queries:, :]
         inverse = 1.0 / sums[cols : cols + 1, :]
         fitted_now = sums[:cols, :] * inverse
+        once = gram[0, :queries, :] + gram[1, :queries, :]
+        gram_high, gram_low = split(0.5 * (once + once.T))
 
         pieces = []
         for h in range(HALVES):
@@ -512,9 +520,8 @@
             pltpu.VMEM((HALVES, 4, 4, 128), F32),
             pltpu.VMEM((queries, n * kept), F32),
             pltpu.VMEM((queries, 128), F32),
-            pltpu.VMEM((2, queries, n * kept), BF16),
-            pltpu.VMEM((cols + 16, n * kept), BF16),
-            pltpu.VMEM((2, queries, queries), F32),
+            pltpu.VMEM((2, queries + cols + 16, n * kept), BF16),
+            pltpu.VMEM((2, queries + cols + 16, queries), F32),
             pltpu.VMEM((n, cols, kept), jnp.int16),
             pltpu.VMEM((head, kept), jnp.int16),
             pltpu.VMEM((n, kept // 128, 128), F32),

time: 64.5 us -> 63.3 us (0.981)
  the two profiles are of different devices: /device:TPU:48 before, /device:TPU:56 now
where the time goes in v4:
time: 63.3 us; the launch traced here: 63.1 us
  Pallas kernels  61.5 us (97%)
  local copies, waits for them, and re-layouts  1.57 us (2%)
    pallas_call x1, Pallas kernels, local(): pl.pallas_call(functools.partial(kernel, n), out_shape=jax.ShapeDtypeStru...  61.5 us
    unnamed x1, local copies, waits for them, and re-layouts  1.57 us

profile of v4, /device:TPU:56, one launch (start us, length us, event | category | flops | bytes accessed | tf_op | source)
XLA Modules:
  0.0 63.1 jit_solution(13717848731621211277)
XLA Ops:
  0.0 61.5 %shard_map.55 = f32[1,256,128]{2,1,0:T(8,128)} custom-call(bf16[1,4096,128]{2,1,0:T(8,128)(2,1)} %keys_hbm.1, bf16[1,4096,128]{2,1,0:T(8,128)(2,1)} %vals_hbm.1, bf16[1,256,128]{2,1,0:T(8,128)(2,1)} %pool_hbm.1, s32[1,256]{1,0:T(1,128)} %kept_hbm.1, s32[1,512]{1,0:T(1,128)} %ref_hbm.1), custom_call_target="tpu_custom_call" | custom-call | tf_op jit(solution)/shard_map/pallas_call | solution.py:492
  61.6 1.6 %copy.7 = f32[1,256,128]{2,1,0:T(8,128)} copy(f32[1,256,128]{2,1,0:T(8,128)} %shard_map.55) | data formatting | bytes 262144

commit v5 on v4

--- a/solution.py
+++ b/solution.py
@@ -106,11 +106,11 @@
 
     barrier = pltpu.get_barrier_semaphore()
 
-    def greet(d, carry):
-        pl.semaphore_signal(barrier, inc=1, device_id=peer(d), device_id_type=MESH)
+    def greet(i, carry):
+        pl.semaphore_signal(barrier, inc=1, device_id=peer(far_first(i)), device_id_type=MESH)
         return carry
 
-    lax.fori_loop(1, n, greet, 0)
+    lax.fori_loop(0, n - 1, greet, 0)
 
     loads = [
         pltpu.make_async_copy(src, dst, load_sem.at[2 + i])
@@ -220,7 +220,7 @@
         def _():
             to_owners(send_kept, keep_kept)
 
-        @pl.when(h == 1)
+        @pl.when(h == core)
         def _():
             to_owners(send_vals, keep_vals)
 

time: 63.3 us -> 63.2 us (level)
  the two profiles are of different devices: /device:TPU:56 before, /device:TPU:20 now
where the time goes in v5:
time: 63.2 us; the launch traced here: 63 us
  Pallas kernels  61.4 us (97%)
  local copies, waits for them, and re-layouts  1.57 us (2%)
    pallas_call x1, Pallas kernels, local(): pl.pallas_call(functools.partial(kernel, n), out_shape=jax.ShapeDtypeStru...  61.4 us
    unnamed x1, local copies, waits for them, and re-layouts  1.57 us

profile of v5, /device:TPU:20, one launch (start us, length us, event | category | flops | bytes accessed | tf_op | source)
XLA Modules:
  0.0 63.0 jit_solution(11295238946031555422)
XLA Ops:
  0.0 61.4 %shard_map.55 = f32[1,256,128]{2,1,0:T(8,128)} custom-call(bf16[1,4096,128]{2,1,0:T(8,128)(2,1)} %keys_hbm.1, bf16[1,4096,128]{2,1,0:T(8,128)(2,1)} %vals_hbm.1, bf16[1,256,128]{2,1,0:T(8,128)(2,1)} %pool_hbm.1, s32[1,256]{1,0:T(1,128)} %kept_hbm.1, s32[1,512]{1,0:T(1,128)} %ref_hbm.1), custom_call_target="tpu_custom_call" | custom-call | tf_op jit(solution)/shard_map/pallas_call | solution.py:492
  61.4 1.6 %copy.7 = f32[1,256,128]{2,1,0:T(8,128)} copy(f32[1,256,128]{2,1,0:T(8,128)} %shard_map.55) | data formatting | bytes 262144
